TPU v7x, 512 devices: a whole 4x8x8 slice. The times are simulated.
512 devices in a mesh: blk: 32 (over y_hi, x, core), fsdp: 16 (over z, y_lo).
Axes of the slice: x: 4, y: 8 (y_hi: 4, y_lo: 2; y = y_hi * 2 + y_lo), z: 8, core: 2. Of those that a mesh axis runs over, the one named last changes fastest.
Arguments:
- weights: bfloat16 [32, 12288, 1536], P('blk', 'fsdp'), may hold values from -9 to 9
- hidden: bfloat16 [32, 256, 12288], P('blk', None, 'fsdp'), may hold values from -6 to 6
- out_grad: bfloat16 [32, 256, 1536], P('blk', 'fsdp'), may hold values from -6 to 6
- q_start: float32 [32, 1536, 4], P('blk'), may hold values from -6 to 6
Outputs:
- new_weights: bfloat16 [32, 12288, 1536], P('blk', 'fsdp')
- edge_factors: float32 [32, 1536, 4], P('blk')
All inputs are finite; a program needn't handle non-finite values.
Results may differ from a plain program's by a relative error of at most 0.013.
Values may be sent and summed in bfloat16 or wider, within the bound.
A program may use at most 64 MiB of HBM per device.

v0:
```python
import math

import jax
import jax.numpy as jnp
from jax import lax
from jax.sharding import PartitionSpec as P

ROUNDS = 2


highest = lax.Precision.HIGHEST


def shifted(block, axis, distance):
    devices = range(lax.axis_size(axis))
    route = [((i - distance) % len(devices), i) for i in devices]
    return lax.ppermute(block, axis, route)


def neighbours(right_term, left_term):
    from_right = shifted(left_term, "blk", -1)
    from_left = shifted(right_term, "blk", 1)
    return (from_right, from_left)


def orthonormal(factor_pair):
    columns = []
    for k in range(factor_pair.shape[-1]):
        vector = factor_pair[..., k]
        if k > 0:
            earlier = jnp.stack(columns, axis=-1)
            coefficients = lax.psum(
                jnp.einsum("efk,ef->ek", earlier, vector, precision=highest), "fsdp"
            )
            vector = vector - jnp.einsum("efk,ek->ef", earlier, coefficients, precision=highest)
        length = lax.psum(jnp.sum(vector * vector, axis=1), "fsdp")
        columns.append(vector / jnp.sqrt(length)[:, None])
    result = jnp.stack(columns, axis=-1)
    return result


def on_device(weights, hidden, out_grad, q_start):
    local_weight = weights[0]
    local_hidden = hidden[0]
    gradient = lax.dot_general(
        local_hidden,
        lax.all_gather(out_grad[0], "fsdp", axis=0, tiled=True),
        (((0,), (0,)), ((), ())),
        preferred_element_type=jnp.float32,
    )
    params = local_weight.astype(jnp.float32) - 0.5 / math.sqrt(local_hidden.shape[0]) * gradient
    q_right = q_start[0]
    q_left = shifted(q_right, "blk", 1)
    factor_pair = None
    for round_index in range(ROUNDS):
        own_right = jnp.dot(params, q_right, precision=highest)
        own_left = jnp.dot(params, q_left, precision=highest)
        from_right, from_left = neighbours(own_right, own_left)
        factor_pair = orthonormal(jnp.stack([own_right - from_right, from_left - own_left]))
        part_right = lax.dot_general(
            params, factor_pair[0], (((0,), (0,)), ((), ())), precision=highest
        )
        part_left = lax.dot_general(
            params, factor_pair[1], (((0,), (0,)), ((), ())), precision=highest
        )
        summed_own = lax.psum(
            jnp.stack([part_right, part_left]).astype(jnp.bfloat16), "fsdp"
        ).astype(jnp.float32)
        back_right, back_left = neighbours(summed_own[0], summed_own[1])
        summed = jnp.stack([summed_own[0] - back_right, back_left - summed_own[1]])
        q_right = summed[0]
        q_left = summed[1]
    update = (
        params
        - 0.5 * jnp.dot(factor_pair[0], q_right.T, precision=highest)
        + 0.5 * jnp.dot(factor_pair[1], q_left.T, precision=highest)
    )
    return (update.astype(jnp.bfloat16)[None], q_right[None])


def solution(mesh):
    placed = (
        P("blk", "fsdp", None),
        P("blk", None, "fsdp"),
        P("blk", "fsdp", None),
        P("blk", None, None),
    )
    return jax.shard_map(
        on_device,
        mesh=mesh,
        in_specs=placed,
        out_specs=(P("blk", "fsdp", None), P("blk", None, None)),
        check_vma=False,
    )
```

profile of v0, /device:TPU:23, one launch (start us, length us, event | category | flops | bytes accessed | tf_op | source)
XLA Modules:
  0.0 714.0 jit_solution(15731538601601926746)
XLA Ops:
  0.7 6.0 collective-permute-start
  6.7 40.2 %all-gather = bf16[1,256,1536]{2,1,0:T(8,128)(2,1)S(1)} all-gather(bf16[1,16,1536]{2,1,0:T(8,128)(2,1)} %param.6), channel_id=2, replica_groups=mesh['blk'=32,'fsdp'=16] {'fsdp'}, dimensions={1}, use_global_device_ids=true | all-gather | bytes 835584 | tf_op jit(solution)/shard_map/all_gather | solution.py:47
  49.4 4.0 fusion.54
  53.4 9.2 %collective-permute-start.2 = (f32[768,4]{0,1:T(4,128)S(1)}, f32[768,4]{0,1:T(4,128)S(1)}, u32[]{:S(2)}, u32[]{:S(2)}) collective-permute-start(f32[768,4]{0,1:T(4,128)S(1)} %fusion.54), channel_id=1, source_target_pairs={{496,0},{0,16},{16,32},{32,48},{48,64},{64,80},{80,96},{96,112},{1... | collective-permute-start | bytes 36872 | tf_op jit(solution)/shard_map/ppermute | solution.py:17
  62.6 4.0 fusion.60
  68.6 7.3 %collective-permute-done.1 = f32[768,4]{0,1:T(4,128)S(1)} collective-permute-done((f32[768,4]{0,1:T(4,128)S(1)}, f32[768,4]{0,1:T(4,128)S(1)}, u32[]{:S(2)}, u32[]{:S(2)}) %collective-permute-start.1) | collective-permute-done | bytes 12320 | tf_op jit(solution)/shard_map/ppermute | solution.py:17
  76.0 23.9 %psum.112 = f32[2]{0:T(128)S(1)} all-reduce(f32[2]{0:T(128)S(1)} %multiply_reduce_fusion.7), channel_id=1, replica_groups=mesh['blk'=32,'fsdp'=16] {'fsdp'}, use_global_device_ids=true, to_apply=%region_1.0 | all-reduce | flops 2 | bytes 16 | tf_op jit(solution)/shard_map/psum | solution.py:36
  100.1 25.5 %psum.113 = f32[2]{0:T(128)S(1)} all-reduce(f32[2]{0:T(128)S(1)} %get-tuple-element.8), channel_id=1, replica_groups=mesh['blk'=32,'fsdp'=16] {'fsdp'}, use_global_device_ids=true, to_apply=%region_2.0 | all-reduce | flops 2 | bytes 16 | tf_op jit(solution)/shard_map/psum | solution.py:32
  125.8 23.9 %psum.114 = f32[2]{0:T(128)S(1)} all-reduce(f32[2]{0:T(128)S(1)} %get-tuple-element.6), channel_id=1, replica_groups=mesh['blk'=32,'fsdp'=16] {'fsdp'}, use_global_device_ids=true, to_apply=%region_4.0 | all-reduce | flops 2 | bytes 16 | tf_op jit(solution)/shard_map/psum | solution.py:36
  150.0 25.6 %psum.115 = f32[2,2]{1,0:T(2,128)S(1)} all-reduce(f32[2,2]{1,0:T(2,128)S(1)} %bitcast.208), channel_id=1, replica_groups=mesh['blk'=32,'fsdp'=16] {'fsdp'}, use_global_device_ids=true, to_apply=%region_5.0 | all-reduce | flops 4 | bytes 32 | tf_op jit(solution)/shard_map/psum | solution.py:32
  175.9 23.8 %psum.116 = f32[2]{0:T(128)S(1)} all-reduce(f32[2]{0:T(128)S(1)} %multiply_reduce_fusion.5), channel_id=1, replica_groups=mesh['blk'=32,'fsdp'=16] {'fsdp'}, use_global_device_ids=true, to_apply=%region_7.0 | all-reduce | flops 2 | bytes 16 | tf_op jit(solution)/shard_map/psum | solution.py:36
  200.0 25.3 %psum.117 = f32[2,3]{1,0:T(2,128)S(1)} all-reduce(f32[2,3]{1,0:T(2,128)S(1)} %bitcast.209), channel_id=1, replica_groups=mesh['blk'=32,'fsdp'=16] {'fsdp'}, use_global_device_ids=true, to_apply=%region_8.0 | all-reduce | flops 6 | bytes 48 | tf_op jit(solution)/shard_map/psum | solution.py:32
  225.6 24.3 %psum.118 = f32[2]{0:T(128)S(1)} all-reduce(f32[2]{0:T(128)S(1)} %multiply_reduce_fusion.4), channel_id=1, replica_groups=mesh['blk'=32,'fsdp'=16] {'fsdp'}, use_global_device_ids=true, to_apply=%region_10.0 | all-reduce | flops 2 | bytes 16 | tf_op jit(solution)/shard_map/psum | solution.py:36
  250.1 5.0 fusion.1
  257.6 48.5 %psum.119 = bf16[2,1536,4]{1,2,0:T(4,128)(2,1)S(1)} all-reduce(bf16[2,1536,4]{1,2,0:T(4,128)(2,1)S(1)} %pad_maximum_fusion.1), channel_id=1, replica_groups=mesh['blk'=32,'fsdp'=16] {'fsdp'}, use_global_device_ids=true, to_apply=%region_11.0 | all-reduce | flops 12288 | bytes 49152 | tf_op jit(solution)/shard_map/psum | solution.py:66
  306.1 65.0 %collective-permute-start.4 = (f32[1536,4]{0,1:T(4,128)S(1)}, f32[1536,4]{0,1:T(4,128)S(1)}, u32[]{:S(2)}, u32[]{:S(2)}) collective-permute-start(f32[1536,4]{0,1:T(4,128)S(1)} %get-tuple-element.12), channel_id=1, source_target_pairs={{496,0},{0,16},{16,32},{32,48},{48,64},{64,80},{80,96},{96,112},{1... | collective-permute-start | bytes 73736 | tf_op jit(solution)/shard_map/ppermute | solution.py:17
  373.1 6.3 fusion.16
  381.3 6.3 fusion.18
  387.5 8.1 %collective-permute-start.6 = (f32[768,4]{0,1:T(4,128)S(1)}, f32[768,4]{0,1:T(4,128)S(1)}, u32[]{:S(2)}, u32[]{:S(2)}) collective-permute-start(f32[768,4]{0,1:T(4,128)S(1)} %fusion.18), channel_id=1, source_target_pairs={{496,0},{0,16},{16,32},{32,48},{48,64},{64,80},{80,96},{96,112},{1... | collective-permute-start | bytes 36872 | tf_op jit(solution)/shard_map/ppermute | solution.py:17
  396.4 24.1 %psum.120 = f32[2]{0:T(128)S(1)} all-reduce(f32[2]{0:T(128)S(1)} %multiply_reduce_fusion.3), channel_id=1, replica_groups=mesh['blk'=32,'fsdp'=16] {'fsdp'}, use_global_device_ids=true, to_apply=%region_13.0 | all-reduce | flops 2 | bytes 16 | tf_op jit(solution)/shard_map/psum | solution.py:36
  420.7 25.0 %psum.121 = f32[2]{0:T(128)S(1)} all-reduce(f32[2]{0:T(128)S(1)} %get-tuple-element.4), channel_id=1, replica_groups=mesh['blk'=32,'fsdp'=16] {'fsdp'}, use_global_device_ids=true, to_apply=%region_14.0 | all-reduce | flops 2 | bytes 16 | tf_op jit(solution)/shard_map/psum | solution.py:32
  445.9 24.4 %psum.122 = f32[2]{0:T(128)S(1)} all-reduce(f32[2]{0:T(128)S(1)} %get-tuple-element.2), channel_id=1, replica_groups=mesh['blk'=32,'fsdp'=16] {'fsdp'}, use_global_device_ids=true, to_apply=%region_16.0 | all-reduce | flops 2 | bytes 16 | tf_op jit(solution)/shard_map/psum | solution.py:36
  470.6 25.2 %psum.123 = f32[2,2]{1,0:T(2,128)S(1)} all-reduce(f32[2,2]{1,0:T(2,128)S(1)} %bitcast.210), channel_id=1, replica_groups=mesh['blk'=32,'fsdp'=16] {'fsdp'}, use_global_device_ids=true, to_apply=%region_17.0 | all-reduce | flops 4 | bytes 32 | tf_op jit(solution)/shard_map/psum | solution.py:32
  496.1 24.4 %psum.124 = f32[2]{0:T(128)S(1)} all-reduce(f32[2]{0:T(128)S(1)} %multiply_reduce_fusion.1), channel_id=1, replica_groups=mesh['blk'=32,'fsdp'=16] {'fsdp'}, use_global_device_ids=true, to_apply=%region_19.0 | all-reduce | flops 2 | bytes 16 | tf_op jit(solution)/shard_map/psum | solution.py:36
  520.9 24.7 %psum.125 = f32[2,3]{1,0:T(2,128)S(1)} all-reduce(f32[2,3]{1,0:T(2,128)S(1)} %bitcast.211), channel_id=1, replica_groups=mesh['blk'=32,'fsdp'=16] {'fsdp'}, use_global_device_ids=true, to_apply=%region_20.0 | all-reduce | flops 6 | bytes 48 | tf_op jit(solution)/shard_map/psum | solution.py:32
  545.9 24.4 %psum.126 = f32[2]{0:T(128)S(1)} all-reduce(f32[2]{0:T(128)S(1)} %multiply_reduce_fusion), channel_id=1, replica_groups=mesh['blk'=32,'fsdp'=16] {'fsdp'}, use_global_device_ids=true, to_apply=%region_22.0 | all-reduce | flops 2 | bytes 16 | tf_op jit(solution)/shard_map/psum | solution.py:36
  570.4 4.8 fusion.4
  575.3 4.8 fusion.3
  580.1 47.2 %psum.127 = bf16[2,1536,4]{1,2,0:T(4,128)(2,1)S(1)} all-reduce(bf16[2,1536,4]{1,2,0:T(4,128)(2,1)S(1)} %pad_maximum_fusion.3), channel_id=1, replica_groups=mesh['blk'=32,'fsdp'=16] {'fsdp'}, use_global_device_ids=true, to_apply=%region_23.0 | all-reduce | flops 12288 | bytes 49152 | tf_op jit(solution)/shard_map/psum | solution.py:66
  627.4 60.6 %collective-permute-start.7 = (f32[1536,4]{0,1:T(4,128)S(1)}, f32[1536,4]{0,1:T(4,128)S(1)}, u32[]{:S(2)}, u32[]{:S(2)}) collective-permute-start(f32[1536,4]{0,1:T(4,128)S(1)} %get-tuple-element.11), channel_id=1, source_target_pairs={{16,0},{32,16},{48,32},{64,48},{80,64},{96,80},{112,96},{128,112},... | collective-permute-start | bytes 73736 | tf_op jit(solution)/shard_map/ppermute | solution.py:17
  688.0 14.1 %collective-permute-start.8 = (f32[1536,4]{0,1:T(4,128)S(1)}, f32[1536,4]{0,1:T(4,128)S(1)}, u32[]{:S(2)}, u32[]{:S(2)}) collective-permute-start(f32[1536,4]{0,1:T(4,128)S(1)} %get-tuple-element.10), channel_id=1, source_target_pairs={{496,0},{0,16},{16,32},{32,48},{48,64},{64,80},{80,96},{96,112},{1... | collective-permute-start | bytes 73736 | tf_op jit(solution)/shard_map/ppermute | solution.py:17
  706.6 7.4 %fusion = bf16[1,768,1536]{2,1,0:T(8,128)(2,1)} fusion(f32[768,1536]{1,0:T(8,128)} %copy-done.1, f32[768,1536]{1,0:T(8,128)S(1)} %fusion.22, f32[1536,4]{0,1:T(4,128)S(1)} %collective-permute-done.8, f32[1,768,4]{1,0,2:T(1,128)S(1)} %get-tuple-element.14, f32[2,1536,4]{1,2,0:T(4,128)S(1)} %convert_element_type.20), kind=kOutput, calls=%fused_computation.2 | convolution fusion | flops 62527488 | bytes 11857920 | tf_op jit(solution)/shard_map/dot_general | solution.py:76
  (75 shorter events, 19.7 us)
Async XLA Ops:
  0.6 46.3 %copy-start = (bf16[1,256,768]{2,1,0:T(8,128)(2,1)S(1)}, bf16[1,256,768]{2,1,0:T(8,128)(2,1)}, u32[]{:S(2)}) copy-start(bf16[1,256,768]{2,1,0:T(8,128)(2,1)} %param.5) | copy-start | bytes 1179652
  0.6 48.8 %copy-start.3 = (f32[1,1536,4]{1,2,0:T(4,128)S(1)}, f32[1,1536,4]{1,2,0:T(4,128)}, u32[]{:S(2)}) copy-start(f32[1,1536,4]{1,2,0:T(4,128)} %param.7) | copy-start | bytes 73732
  0.7 62.0 %collective-permute-start = (f32[1536,4]{0,1:T(4,128)}, f32[1536,4]{0,1:T(4,128)S(1)}, u32[]{:S(2)}, u32[]{:S(2)}) collective-permute-start(f32[1536,4]{0,1:T(4,128)} %bitcast.203), channel_id=1, source_target_pairs={{496,0},{0,16},{16,32},{32,48},{48,64},{64,80},{80,96},{96,112},{1... | collective-permute-start | bytes 73736 | tf_op jit(solution)/shard_map/ppermute | solution.py:17
  49.4 17.2 %copy-start.1 = (f32[768,1536]{1,0:T(8,128)}, f32[768,1536]{1,0:T(8,128)S(1)}, u32[]{:S(2)}) copy-start(f32[768,1536]{1,0:T(8,128)S(1)} %convert_subtract_fusion) | copy-start | bytes 14155780
  53.4 15.2 %collective-permute-start.2 = (f32[768,4]{0,1:T(4,128)S(1)}, f32[768,4]{0,1:T(4,128)S(1)}, u32[]{:S(2)}, u32[]{:S(2)}) collective-permute-start(f32[768,4]{0,1:T(4,128)S(1)} %fusion.54), channel_id=1, source_target_pairs={{496,0},{0,16},{16,32},{32,48},{48,64},{64,80},{80,96},{96,112},{1... | collective-permute-start | bytes 36872 | tf_op jit(solution)/shard_map/ppermute | solution.py:17
  66.6 9.2 %collective-permute-start.1 = (f32[768,4]{0,1:T(4,128)S(1)}, f32[768,4]{0,1:T(4,128)S(1)}, u32[]{:S(2)}, u32[]{:S(2)}) collective-permute-start(f32[768,4]{0,1:T(4,128)S(1)} %fusion.60), channel_id=1, source_target_pairs={{16,0},{32,16},{48,32},{64,48},{80,64},{96,80},{112,96},{128,112},... | collective-permute-start | bytes 36872 | tf_op jit(solution)/shard_map/ppermute | solution.py:17
  249.9 5.1 copy-start.2
  306.1 66.9 %collective-permute-start.4 = (f32[1536,4]{0,1:T(4,128)S(1)}, f32[1536,4]{0,1:T(4,128)S(1)}, u32[]{:S(2)}, u32[]{:S(2)}) collective-permute-start(f32[1536,4]{0,1:T(4,128)S(1)} %get-tuple-element.12), channel_id=1, source_target_pairs={{496,0},{0,16},{16,32},{32,48},{48,64},{64,80},{80,96},{96,112},{1... | collective-permute-start | bytes 73736 | tf_op jit(solution)/shard_map/ppermute | solution.py:17
  371.1 10.1 %collective-permute-start.3 = (f32[1536,4]{0,1:T(4,128)S(1)}, f32[1536,4]{0,1:T(4,128)S(1)}, u32[]{:S(2)}, u32[]{:S(2)}) collective-permute-start(f32[1536,4]{0,1:T(4,128)S(1)} %get-tuple-element.13), channel_id=1, source_target_pairs={{16,0},{32,16},{48,32},{64,48},{80,64},{96,80},{112,96},{128,112},... | collective-permute-start | bytes 73736 | tf_op jit(solution)/shard_map/ppermute | solution.py:17
  379.3 16.3 %collective-permute-start.5 = (f32[768,4]{0,1:T(4,128)S(1)}, f32[768,4]{0,1:T(4,128)S(1)}, u32[]{:S(2)}, u32[]{:S(2)}) collective-permute-start(f32[768,4]{0,1:T(4,128)S(1)} %fusion.16), channel_id=1, source_target_pairs={{16,0},{32,16},{48,32},{64,48},{80,64},{96,80},{112,96},{128,112},... | collective-permute-start | bytes 36872 | tf_op jit(solution)/shard_map/ppermute | solution.py:17
  387.5 8.7 %collective-permute-start.6 = (f32[768,4]{0,1:T(4,128)S(1)}, f32[768,4]{0,1:T(4,128)S(1)}, u32[]{:S(2)}, u32[]{:S(2)}) collective-permute-start(f32[768,4]{0,1:T(4,128)S(1)} %fusion.18), channel_id=1, source_target_pairs={{496,0},{0,16},{16,32},{32,48},{48,64},{64,80},{80,96},{96,112},{1... | collective-permute-start | bytes 36872 | tf_op jit(solution)/shard_map/ppermute | solution.py:17
  627.4 74.7 %collective-permute-start.7 = (f32[1536,4]{0,1:T(4,128)S(1)}, f32[1536,4]{0,1:T(4,128)S(1)}, u32[]{:S(2)}, u32[]{:S(2)}) collective-permute-start(f32[1536,4]{0,1:T(4,128)S(1)} %get-tuple-element.11), channel_id=1, source_target_pairs={{16,0},{32,16},{48,32},{64,48},{80,64},{96,80},{112,96},{128,112},... | collective-permute-start | bytes 73736 | tf_op jit(solution)/shard_map/ppermute | solution.py:17
  688.0 18.6 %collective-permute-start.8 = (f32[1536,4]{0,1:T(4,128)S(1)}, f32[1536,4]{0,1:T(4,128)S(1)}, u32[]{:S(2)}, u32[]{:S(2)}) collective-permute-start(f32[1536,4]{0,1:T(4,128)S(1)} %get-tuple-element.10), channel_id=1, source_target_pairs={{496,0},{0,16},{16,32},{32,48},{48,64},{64,80},{80,96},{96,112},{1... | collective-permute-start | bytes 73736 | tf_op jit(solution)/shard_map/ppermute | solution.py:17
where the time goes:
time: 715 us; the launch traced here: 714 us
  blocking collectives  480 us (67%)
  starting transfers between devices  169 us (24%)
  matrix products  52.9 us (7%)
  waiting for transfers between devices  7.86 us (1%)
    psum x8, blocking collectives, orthonormal(): length = lax.psum(jnp.sum(vector * vector, axis=1), 'fsdp')  193 us
    ppermute x9, starting transfers between devices, shifted(): return lax.ppermute(block, axis, route)  169 us
    psum x6, blocking collectives, orthonormal(): lax.psum(jnp.einsum('efk,ef->ek', earlier, vector, precision=highest), 'f...  151 us
    psum x2, blocking collectives, on_device(): lax.psum(jnp.stack([part_right, part_left]).astype(jnp.bfloat16), 'fsdp')  95.7 us
    all_gather x1, blocking collectives, on_device(): lax.all_gather(out_grad[0], 'fsdp', axis=0, tiled=True)  40.2 us
  transfers between devices with their start and end apart: 9, of which 2 were waited for; matrix products, arithmetic and copies ran while one was open for 4% of the time, Pallas kernels for 0%

commit v1 on v0

v1 whole, which is shorter than its diff:
```python
import functools
import math

import jax
import jax.numpy as jnp
from jax import lax
from jax.experimental import pallas as pl
from jax.experimental.pallas import tpu as pltpu
from jax.sharding import PartitionSpec as P

ROUNDS = 2
MESH = pl.DeviceIdType.MESH
F32, BF16 = jnp.float32, jnp.bfloat16

NT = (((1,), (1,)), ((), ()))
NN = (((1,), (0,)), ((), ()))
TN = (((0,), (0,)), ((), ()))


def mm(a, b, dims):
    return lax.dot_general(a, b, dims, preferred_element_type=F32)


def pieces(x):
    high = x.astype(BF16).astype(F32)
    rest = x - high
    mid = rest.astype(BF16).astype(F32)
    low = rest - mid
    return jnp.concatenate([high, mid, low], axis=0).astype(BF16)


def joined(y):
    n = y.shape[0] // 3
    return y[:n] + (y[n : 2 * n] + y[2 * n :])


def edge_row(x, k, first):
    return jnp.where(
        first,
        jnp.broadcast_to(x[k : k + 1], x.shape),
        jnp.broadcast_to(x[4 + k : 5 + k], x.shape),
    )


def eliminate(q, m, others):
    rows = lax.broadcasted_iota(jnp.int32, (8, 1), 0)
    first = rows < 4
    within = rows - jnp.where(first, 0, 4)
    gram = [jnp.sum(m * edge_row(q, k, first), axis=1, keepdims=True) for k in range(4)]
    arrays = [m] + others
    diagonal = jnp.zeros((8, 1), F32)
    for k in range(4):
        pivot = edge_row(gram[k], k, first)
        diagonal = jnp.where(within == k, gram[k], diagonal)
        factor = jnp.where(within > k, gram[k] / pivot, 0.0)
        if k < 3:
            for j in range(k + 1, 4):
                gram[j] = gram[j] - factor * edge_row(gram[j], k, first)
            arrays = [a - factor * edge_row(a, k, first) for a in arrays]
    scale = 1.0 / jnp.sqrt(diagonal)
    return [a * scale for a in arrays]


def kernel(n_blk, n_fsdp, step, w_hbm, h_hbm, g_hbm, q_hbm, new_hbm, edge_ref,
           w, h, g, base, out, g_ref, q_ref, q_left, q_all, p_send, p_recv, m_part, m_recv, m_sum,
           x_send, x_recv, in_sem, out_sem, q_sem, g_sem, p_sem, rs_sem, ag_sem, x_sem):
    b, f = lax.axis_index("blk"), lax.axis_index("fsdp")
    up, down = lax.rem(b + 1, n_blk), lax.rem(b + n_blk - 1, n_blk)
    half = n_fsdp // 2
    mine = lax.rem(f, half)
    start_of_half = f - mine
    rows, width = w.shape
    strip = width // (half // 2)

    def remote(src, dst, sems, at, where):
        return pltpu.make_async_remote_copy(
            src_ref=src, dst_ref=dst, send_sem=sems.at[at], recv_sem=sems.at[at + 1],
            device_id=where, device_id_type=MESH,
        )

    def settle(ref, sem):
        pltpu.make_async_copy(ref, ref, sem).wait()

    load_w = pltpu.make_async_copy(w_hbm, w, in_sem.at[0])
    load_h = pltpu.make_async_copy(h_hbm, h, in_sem.at[1])
    load_g = pltpu.make_async_copy(g_hbm, g_ref, in_sem.at[2])
    load_q = pltpu.make_async_copy(q_hbm, q_ref, in_sem.at[3])
    for load in (load_q, load_g, load_w, load_h):
        load.start()
    others = [(b, lax.rem(f + k, n_fsdp)) for k in range(1, n_fsdp)]
    barrier = pltpu.get_barrier_semaphore()
    for where in others + [(up, f), (down, f)]:
        pl.semaphore_signal(barrier, inc=1, device_id=where, device_id_type=MESH)
    pl.semaphore_wait(barrier, n_fsdp + 1)

    load_q.wait()
    load_g.wait()
    send_q = remote(q_ref, q_left, q_sem, 0, (up, f))
    send_q.start()
    for where in others:
        remote(g_ref, g.at[f], g_sem, 0, where).start()
    g[f] = g_ref[...]
    q_all[0:4] = q_ref[...]
    load_w.wait()
    load_h.wait()
    send_q.wait_recv()
    q_all[4:8] = q_left[...]
    q = q_all[...]

    def gather_g():
        settle(g.at[pl.ds(0, n_fsdp - 1)], g_sem.at[1])

    for r in range(ROUNDS):
        q3 = pieces(q)
        own = joined(mm(q3, w[...], NT))
        if r == 0:
            gather_g()
        tokens = g[...].reshape(n_fsdp * g.shape[1], width)
        own = own - joined(mm(pieces(step * joined(mm(q3, tokens, NT))), h[...], NN))
        p_send[r, 0] = own[0:4]
        p_send[r, 1] = own[4:8]
        to_up = remote(p_send.at[r, 0], p_recv.at[r, 1], p_sem, 4 * r, (up, f))
        to_down = remote(p_send.at[r, 1], p_recv.at[r, 0], p_sem, 4 * r + 2, (down, f))
        to_up.start()
        to_down.start()
        if r == 0:
            for i in range(0, rows, 128):
                base[i : i + 128] = w[i : i + 128].astype(F32) - step * mm(h[:, i : i + 128], tokens, TN)
        to_up.wait_recv()
        to_down.wait_recv()
        p = jnp.concatenate([own[0:4] - p_recv[r, 0], p_recv[r, 1] - own[4:8]], axis=0)
        p3 = pieces(p)
        part = joined(mm(p3, w[...], NN))
        part = part - joined(mm(pieces(step * joined(mm(p3, h[...], NT))), tokens, NN))
        for s in range(half):
            i, j = 4 * (s // (half // 2)), strip * (s % (half // 2))
            m_part[r, s] = part[i : i + 4, j : j + strip]
        for k in range(1, half):
            to = lax.rem(mine + k, half)
            remote(m_part.at[r, to], m_recv.at[r, mine], rs_sem, 2 * r, (b, start_of_half + to)).start()
        m_recv[r, mine] = m_part[r, mine]
        settle(m_recv.at[r, pl.ds(0, half - 1)], rs_sem.at[2 * r + 1])
        total = m_recv[r, 0]
        for s in range(1, half):
            total = total + m_recv[r, s]
        m_sum[r, f] = total
        for where in others:
            remote(m_sum.at[r, f], m_sum.at[r, f], ag_sem, 2 * r, where).start()
        settle(m_sum.at[r, pl.ds(0, n_fsdp - 1)], ag_sem.at[2 * r + 1])
        for s in range(half):
            e, j = s // (half // 2), strip * (s % (half // 2))
            x_send[r, e, :, j : j + strip] = m_sum[r, s] + m_sum[r, half + s]
        to_up = remote(x_send.at[r, 0], x_recv.at[r, 1], x_sem, 4 * r, (up, f))
        to_down = remote(x_send.at[r, 1], x_recv.at[r, 0], x_sem, 4 * r + 2, (down, f))
        to_up.start()
        to_down.start()
        to_up.wait_recv()
        to_down.wait_recv()
        m = jnp.concatenate(
            [x_send[r, 0] - x_recv[r, 0], x_recv[r, 1] - x_send[r, 1]], axis=0
        )
        if r < ROUNDS - 1:
            (q,) = eliminate(q, m, [])
        else:
            q, p = eliminate(q, m, [p])

    edge_ref[...] = q[0:4]
    sign = jnp.where(lax.broadcasted_iota(jnp.int32, (8, 1), 0) < 4, -0.5, 0.5)
    q3, p3 = pieces(q), pieces(sign * p)
    left = jnp.concatenate([p3[0:8], p3[0:8], p3[8:16], p3[0:8], p3[16:24], p3[8:16]], axis=0)
    right = jnp.concatenate([q3[0:8], q3[8:16], q3[0:8], q3[16:24], q3[0:8], q3[8:16]], axis=0)
    saves = []
    for n, i in enumerate(range(0, rows, 128)):
        out[i : i + 128] = (base[i : i + 128] + mm(left[:, i : i + 128], right, TN)).astype(BF16)
        save = pltpu.make_async_copy(out.at[i : i + 128], new_hbm.at[i : i + 128], out_sem.at[n])
        save.start()
        saves.append(save)

    send_q.wait_send()
    settle(g.at[pl.ds(0, n_fsdp - 1)], g_sem.at[0])
    for r in range(ROUNDS):
        settle(p_send.at[r, 0], p_sem.at[4 * r])
        settle(p_send.at[r, 1], p_sem.at[4 * r + 2])
        settle(m_recv.at[r, pl.ds(0, half - 1)], rs_sem.at[2 * r])
        settle(m_sum.at[r, pl.ds(0, n_fsdp - 1)], ag_sem.at[2 * r])
        settle(x_send.at[r, 0], x_sem.at[4 * r])
        settle(x_send.at[r, 1], x_sem.at[4 * r + 2])
    for save in saves:
        save.wait()


def on_device(n_blk, n_fsdp, weights, hidden, out_grad, q_start):
    w, h, g, q = weights[0], hidden[0], out_grad[0], q_start[0].T
    rows, width = w.shape
    tokens = h.shape[0]
    rank = q.shape[0]
    half = n_fsdp // 2
    strip = width // (half // 2)
    dma = pltpu.SemaphoreType.DMA
    vmem = pl.BlockSpec(memory_space=pltpu.VMEM)
    hbm = pl.BlockSpec(memory_space=pl.ANY)
    new, edge = pl.pallas_call(
        functools.partial(kernel, n_blk, n_fsdp, 0.5 / math.sqrt(tokens)),
        out_shape=(
            jax.ShapeDtypeStruct((rows, width), BF16),
            jax.ShapeDtypeStruct((rank, width), F32),
        ),
        in_specs=[hbm, hbm, hbm, hbm],
        out_specs=(hbm, vmem),
        scratch_shapes=[
            pltpu.VMEM((rows, width), BF16),
            pltpu.VMEM((tokens, rows), BF16),
            pltpu.VMEM((n_fsdp, tokens // n_fsdp, width), BF16),
            pltpu.VMEM((rows, width), F32),
            pltpu.VMEM((rows, width), BF16),
            pltpu.VMEM((tokens // n_fsdp, width), BF16),
            pltpu.VMEM((rank, width), F32),
            pltpu.VMEM((rank, width), F32),
            pltpu.VMEM((2 * rank, width), F32),
            pltpu.VMEM((ROUNDS, 2, rank, rows), F32),
            pltpu.VMEM((ROUNDS, 2, rank, rows), F32),
            pltpu.VMEM((ROUNDS, half, rank, strip), F32),
            pltpu.VMEM((ROUNDS, half, rank, strip), F32),
            pltpu.VMEM((ROUNDS, n_fsdp, rank, strip), F32),
            pltpu.VMEM((ROUNDS, 2, rank, width), F32),
            pltpu.VMEM((ROUNDS, 2, rank, width), F32),
            dma((4,)),
            dma((rows // 128,)),
            dma((2,)),
            dma((2,)),
            dma((4 * ROUNDS,)),
            dma((2 * ROUNDS,)),
            dma((2 * ROUNDS,)),
            dma((4 * ROUNDS,)),
        ],
        compiler_params=pltpu.CompilerParams(
            collective_id=0, has_side_effects=True, vmem_limit_bytes=60 << 20
        ),
    )(w, h, g, q)
    return new[None], edge.T[None]


def solution(mesh):
    placed = (
        P("blk", "fsdp", None),
        P("blk", None, "fsdp"),
        P("blk", "fsdp", None),
        P("blk", None, None),
    )
    return jax.shard_map(
        functools.partial(on_device, mesh.shape["blk"], mesh.shape["fsdp"]),
        mesh=mesh,
        in_specs=placed,
        out_specs=(P("blk", "fsdp", None), P("blk", None, None)),
        check_vma=False,
    )
```

time: 715 us -> 79.1 us (0.11)
  blocking collectives: 480 us -> 0 us
  starting transfers between devices: 169 us -> 0 us
  Pallas kernels: 0 us -> 74.5 us
  matrix products: 52.9 us -> 0 us
  waiting for transfers between devices: 7.86 us -> 0 us
    psum x16 -> x0, blocking collectives: 440 us -> none  [the longest x8 193 us: orthonormal(): length = lax.psum(jnp.sum(vector * vector, axis=1), 'fsdp')]
    ppermute x9 -> x0, starting transfers between devices: 169 us -> none  [shifted(): return lax.ppermute(block, axis, route)]
    pallas_call x0 -> x1, Pallas kernels: none -> 74.5 us  [on_device(): pl.pallas_call(functools.partial(kernel, n_blk, n_fsdp, 0.5 / math.sqrt(t...]
    dot_general x19 -> x0, matrix products: 52.9 us -> none  [the longest x2 10.2 us: on_device(): own_left = jnp.dot(params, q_left, precision=highest)]
    all_gather x1 -> x0, blocking collectives: 40.2 us -> none  [on_device(): lax.all_gather(out_grad[0], 'fsdp', axis=0, tiled=True)]
    ppermute x9 -> x0, waiting for transfers between devices: 7.86 us -> none  [shifted(): return lax.ppermute(block, axis, route)]
  transfers between devices with their start and end apart: 9 -> 0, of which waited for: 2 -> 0; matrix products, arithmetic and copies ran while one was open for 4% -> 0% of each run, Pallas kernels for 0% -> 0%
where the time goes in v1:
time: 79.1 us; the launch traced here: 78.9 us
  Pallas kernels  74.5 us (94%)
  local copies, waits for them, and re-layouts  3.84 us (5%)
    pallas_call x1, Pallas kernels, on_device(): pl.pallas_call(functools.partial(kernel, n_blk, n_fsdp, 0.5 / math.sqrt(t...  74.5 us
    unnamed x4, local copies, waits for them, and re-layouts  3.84 us

profile of v1, /device:TPU:23, one launch (start us, length us, event | category | flops | bytes accessed | tf_op | source)
XLA Modules:
  0.0 78.9 jit_solution(16179475475216441211)
XLA Ops:
  0.6 74.5 %shard_map.59 = (bf16[768,1536]{1,0:T(8,128)(2,1)}, f32[4,1536]{1,0:T(4,128)}) custom-call(bf16[768,1536]{1,0:T(8,128)(2,1)} %bitcast.10, bf16[256,768]{1,0:T(8,128)(2,1)} %bitcast.12, bf16[16,1536]{1,0:T(8,128)(2,1)} %bitcast.13, f32[4,1536]{1,0:T(4,128)} %bitcast.14), custom_call_target="tpu_custom_call" | custom-call | tf_op jit(solution)/shard_map/pallas_call | solution.py:202
  75.1 0.0 copy-start
  75.1 3.2 %copy.8 = bf16[1,768,1536]{2,1,0:T(8,128)(2,1)} copy(bf16[1,768,1536]{2,1,0:T(8,128)(2,1)} %bitcast.11) | data formatting | bytes 4718592
  78.3 0.0 copy-done
  78.3 0.6 copy.9
Async XLA Ops:
  75.1 3.2 %copy-start = (f32[4,1536]{1,0:T(4,128)S(1)}, f32[4,1536]{1,0:T(4,128)}, u32[]{:S(2)}) copy-start(f32[4,1536]{1,0:T(4,128)} %get-tuple-element.5) | copy-start | bytes 73732

commit v2 on v1

--- a/solution.py
+++ b/solution.py
@@ -61,9 +61,9 @@
     return [a * scale for a in arrays]
 
 
-def kernel(n_blk, n_fsdp, step, w_hbm, h_hbm, g_hbm, q_hbm, new_hbm, edge_ref,
-           w, h, g, base, out, g_ref, q_ref, q_left, q_all, p_send, p_recv, m_part, m_recv, m_sum,
-           x_send, x_recv, in_sem, out_sem, q_sem, g_sem, p_sem, rs_sem, ag_sem, x_sem):
+def kernel(n_blk, n_fsdp, step, w_hbm, h_hbm, g_hbm, q_hbm, base, left, right, edge_ref,
+           w, h, g, g_ref, q_ref, q_left, q_all, p_send, p_recv, m_part, m_recv, m_sum,
+           m_all, in_sem, q_sem, g_sem, p_sem, rs_sem, ag_sem):
     b, f = lax.axis_index("blk"), lax.axis_index("fsdp")
     up, down = lax.rem(b + 1, n_blk), lax.rem(b + n_blk - 1, n_blk)
     half = n_fsdp // 2
@@ -89,9 +89,10 @@
         load.start()
     others = [(b, lax.rem(f + k, n_fsdp)) for k in range(1, n_fsdp)]
     barrier = pltpu.get_barrier_semaphore()
-    for where in others + [(up, f), (down, f)]:
+    beside = [(there, start_of_half + s) for there in (up, down) for s in range(half)]
+    for where in others + beside:
         pl.semaphore_signal(barrier, inc=1, device_id=where, device_id_type=MESH)
-    pl.semaphore_wait(barrier, n_fsdp + 1)
+    pl.semaphore_wait(barrier, len(others) + len(beside))
 
     load_q.wait()
     load_g.wait()
@@ -135,30 +136,25 @@
         for s in range(half):
             i, j = 4 * (s // (half // 2)), strip * (s % (half // 2))
             m_part[r, s] = part[i : i + 4, j : j + strip]
+        for s in range(half // 2):
+            remote(m_part.at[r, s], m_recv.at[r, half + mine], rs_sem, 2 * r, (up, start_of_half + half // 2 + s)).start()
+            remote(m_part.at[r, half // 2 + s], m_recv.at[r, half + mine], rs_sem, 2 * r, (down, start_of_half + s)).start()
         for k in range(1, half):
             to = lax.rem(mine + k, half)
             remote(m_part.at[r, to], m_recv.at[r, mine], rs_sem, 2 * r, (b, start_of_half + to)).start()
         m_recv[r, mine] = m_part[r, mine]
-        settle(m_recv.at[r, pl.ds(0, half - 1)], rs_sem.at[2 * r + 1])
-        total = m_recv[r, 0]
+        settle(m_recv.at[r, pl.ds(0, 2 * half - 1)], rs_sem.at[2 * r + 1])
+        total = m_recv[r, 0] - m_recv[r, half]
         for s in range(1, half):
-            total = total + m_recv[r, s]
-        m_sum[r, f] = total
+            total = total + (m_recv[r, s] - m_recv[r, half + s])
+        m_sum[r, f] = jnp.where(mine < half // 2, 1.0, -1.0) * total
         for where in others:
             remote(m_sum.at[r, f], m_sum.at[r, f], ag_sem, 2 * r, where).start()
         settle(m_sum.at[r, pl.ds(0, n_fsdp - 1)], ag_sem.at[2 * r + 1])
         for s in range(half):
-            e, j = s // (half // 2), strip * (s % (half // 2))
-            x_send[r, e, :, j : j + strip] = m_sum[r, s] + m_sum[r, half + s]
-        to_up = remote(x_send.at[r, 0], x_recv.at[r, 1], x_sem, 4 * r, (up, f))
-        to_down = remote(x_send.at[r, 1], x_recv.at[r, 0], x_sem, 4 * r + 2, (down, f))
-        to_up.start()
-        to_down.start()
-        to_up.wait_recv()
-        to_down.wait_recv()
-        m = jnp.concatenate(
-            [x_send[r, 0] - x_recv[r, 0], x_recv[r, 1] - x_send[r, 1]], axis=0
-        )
+            i, j = 4 * (s // (half // 2)), strip * (s % (half // 2))
+            m_all[i : i + 4, j : j + strip] = m_sum[r, s] + m_sum[r, half + s]
+        m = m_all[...]
         if r < ROUNDS - 1:
             (q,) = eliminate(q, m, [])
         else:
@@ -167,24 +163,26 @@
     edge_ref[...] = q[0:4]
     sign = jnp.where(lax.broadcasted_iota(jnp.int32, (8, 1), 0) < 4, -0.5, 0.5)
     q3, p3 = pieces(q), pieces(sign * p)
-    left = jnp.concatenate([p3[0:8], p3[0:8], p3[8:16], p3[0:8], p3[16:24], p3[8:16]], axis=0)
-    right = jnp.concatenate([q3[0:8], q3[8:16], q3[0:8], q3[16:24], q3[0:8], q3[8:16]], axis=0)
-    saves = []
-    for n, i in enumerate(range(0, rows, 128)):
-        out[i : i + 128] = (base[i : i + 128] + mm(left[:, i : i + 128], right, TN)).astype(BF16)
-        save = pltpu.make_async_copy(out.at[i : i + 128], new_hbm.at[i : i + 128], out_sem.at[n])
-        save.start()
-        saves.append(save)
+    left[...] = jnp.concatenate([p3[0:8], p3[0:8], p3[8:16], p3[0:8], p3[16:24], p3[8:16]], axis=0)
+    right[...] = jnp.concatenate([q3[0:8], q3[8:16], q3[0:8], q3[16:24], q3[0:8], q3[8:16]], axis=0)
 
     send_q.wait_send()
     settle(g.at[pl.ds(0, n_fsdp - 1)], g_sem.at[0])
     for r in range(ROUNDS):
         settle(p_send.at[r, 0], p_sem.at[4 * r])
         settle(p_send.at[r, 1], p_sem.at[4 * r + 2])
-        settle(m_recv.at[r, pl.ds(0, half - 1)], rs_sem.at[2 * r])
+        settle(m_recv.at[r, pl.ds(0, 2 * half - 1)], rs_sem.at[2 * r])
         settle(m_sum.at[r, pl.ds(0, n_fsdp - 1)], ag_sem.at[2 * r])
-        settle(x_send.at[r, 0], x_sem.at[4 * r])
-        settle(x_send.at[r, 1], x_sem.at[4 * r + 2])
+
+
+def write_kernel(base, left, right, edge, new_hbm, edge_hbm, new, sem):
+    saves = [pltpu.make_async_copy(edge, edge_hbm, sem.at[0])]
+    saves[0].start()
+    for n, i in enumerate(range(0, base.shape[0], 128)):
+        at = pl.ds(i, 128)
+        new[at] = (base[at] + mm(left[:, at], right[...], TN)).astype(BF16)
+        saves.append(pltpu.make_async_copy(new.at[at], new_hbm.at[at], sem.at[1 + n]))
+        saves[-1].start()
     for save in saves:
         save.wait()
 
@@ -199,20 +197,20 @@
     dma = pltpu.SemaphoreType.DMA
     vmem = pl.BlockSpec(memory_space=pltpu.VMEM)
     hbm = pl.BlockSpec(memory_space=pl.ANY)
-    new, edge = pl.pallas_call(
+    parts = pl.pallas_call(
         functools.partial(kernel, n_blk, n_fsdp, 0.5 / math.sqrt(tokens)),
         out_shape=(
-            jax.ShapeDtypeStruct((rows, width), BF16),
-            jax.ShapeDtypeStruct((rank, width), F32),
+            pltpu.VMEM((rows, width), F32),
+            pltpu.VMEM((12 * rank, rows), BF16),
+            pltpu.VMEM((12 * rank, width), BF16),
+            pltpu.VMEM((rank, width), F32),
         ),
         in_specs=[hbm, hbm, hbm, hbm],
-        out_specs=(hbm, vmem),
+        out_specs=(vmem, vmem, vmem, vmem),
         scratch_shapes=[
             pltpu.VMEM((rows, width), BF16),
             pltpu.VMEM((tokens, rows), BF16),
             pltpu.VMEM((n_fsdp, tokens // n_fsdp, width), BF16),
-            pltpu.VMEM((rows, width), F32),
-            pltpu.VMEM((rows, width), BF16),
             pltpu.VMEM((tokens // n_fsdp, width), BF16),
             pltpu.VMEM((rank, width), F32),
             pltpu.VMEM((rank, width), F32),
@@ -220,23 +218,31 @@
             pltpu.VMEM((ROUNDS, 2, rank, rows), F32),
             pltpu.VMEM((ROUNDS, 2, rank, rows), F32),
             pltpu.VMEM((ROUNDS, half, rank, strip), F32),
-            pltpu.VMEM((ROUNDS, half, rank, strip), F32),
+            pltpu.VMEM((ROUNDS, 2 * half, rank, strip), F32),
             pltpu.VMEM((ROUNDS, n_fsdp, rank, strip), F32),
-            pltpu.VMEM((ROUNDS, 2, rank, width), F32),
-            pltpu.VMEM((ROUNDS, 2, rank, width), F32),
+            pltpu.VMEM((2 * rank, width), F32),
             dma((4,)),
-            dma((rows // 128,)),
             dma((2,)),
             dma((2,)),
             dma((4 * ROUNDS,)),
             dma((2 * ROUNDS,)),
             dma((2 * ROUNDS,)),
-            dma((4 * ROUNDS,)),
         ],
         compiler_params=pltpu.CompilerParams(
-            collective_id=0, has_side_effects=True, vmem_limit_bytes=60 << 20
+            collective_id=0, has_side_effects=True, vmem_limit_bytes=40 << 20
         ),
-    )(w, h, g, q)
+    )(*(pltpu.with_memory_space_constraint(x, pltpu.HBM) for x in (w, h, g, q)))
+    new, edge = pl.pallas_call(
+        write_kernel,
+        out_shape=(
+            jax.ShapeDtypeStruct((rows, width), BF16),
+            jax.ShapeDtypeStruct((rank, width), F32),
+        ),
+        in_specs=[vmem] * 4,
+        out_specs=(hbm, hbm),
+        scratch_shapes=[pltpu.VMEM((rows, width), BF16), dma((rows // 128 + 1,))],
+        compiler_params=pltpu.CompilerParams(vmem_limit_bytes=16 << 20),
+    )(*(pltpu.with_memory_space_constraint(x, pltpu.VMEM) for x in parts))
     return new[None], edge.T[None]
 
 

time: 79.1 us -> 69.3 us (0.88)
  the two profiles are of different devices: /device:TPU:23 before, /device:TPU:40 now
where the time goes in v2:
time: 69.3 us; the launch traced here: 69.1 us
  Pallas kernels  68.5 us (99%)
    pallas_call x1, Pallas kernels, on_device(): pl.pallas_call(functools.partial(kernel, n_blk, n_fsdp, 0.5 / math.sqrt(t...  66.7 us
    pallas_call x1, Pallas kernels, on_device(): pl.pallas_call(write_kernel, out_shape=(jax.ShapeDtypeStruct((rows, width...  1.74 us

profile of v2, /device:TPU:40, one launch (start us, length us, event | category | flops | bytes accessed | tf_op | source)
XLA Modules:
  0.0 69.1 jit_solution(6171585994603510410)
XLA Ops:
  0.6 66.7 %shard_map.59 = (f32[768,1536]{1,0:T(8,128)S(1)}, bf16[48,768]{1,0:T(8,128)(2,1)S(1)}, bf16[48,1536]{1,0:T(8,128)(2,1)S(1)}, f32[4,1536]{1,0:T(4,128)S(1)}) custom-call(bf16[768,1536]{1,0:T(8,128)(2,1)} %bitcast.10, bf16[256,768]{1,0:T(8,128)(2,1)} %bitcast.11, bf16[16,1536]{1,0:T(8,128)(2,1)} %bitcast.12, f32[4,1536]{1,0:T(4,128)} %bitcast.13), custom_call_target="tpu_custom_call" | custom-call | tf_op jit(solution)/shard_map/pallas_call | solution.py:200
  67.4 1.7 %shard_map.60 = (bf16[768,1536]{1,0:T(8,128)(2,1)}, f32[4,1536]{1,0:T(4,128)}) custom-call(f32[768,1536]{1,0:T(8,128)S(1)} %get-tuple-element.8.base, bf16[48,768]{1,0:T(8,128)(2,1)S(1)} %get-tuple-element.9.left, bf16[48,1536]{1,0:T(8,128)(2,1)S(1)} %get-tuple-element.10.right, f32[4,1536]{1,0:T(4,128)S(1)} %get-tuple-element.11.edge), custom_call_target="tpu_custom_call" | custom-call | tf_op jit(solution)/shard_map/pallas_call | solution.py:235

commit v3 on v2

--- a/solution.py
+++ b/solution.py
@@ -62,8 +62,8 @@
 
 
 def kernel(n_blk, n_fsdp, step, w_hbm, h_hbm, g_hbm, q_hbm, base, left, right, edge_ref,
-           w, h, g, g_ref, q_ref, q_left, q_all, p_send, p_recv, m_part, m_recv, m_sum,
-           m_all, in_sem, q_sem, g_sem, p_sem, rs_sem, ag_sem):
+           w, h, g, g_ref, g_pad, gq, q_ref, q_left, q_all, p_send, p_recv, m_part, m_recv, m_sum,
+           m_all, in_sem, q_sem, gq_sem, g_sem, p_sem, rs_sem, ag_sem):
     b, f = lax.axis_index("blk"), lax.axis_index("fsdp")
     up, down = lax.rem(b + 1, n_blk), lax.rem(b + n_blk - 1, n_blk)
     half = n_fsdp // 2
@@ -98,26 +98,37 @@
     load_g.wait()
     send_q = remote(q_ref, q_left, q_sem, 0, (up, f))
     send_q.start()
-    for where in others:
-        remote(g_ref, g.at[f], g_sem, 0, where).start()
+    line = [lax.rem(f + 2 * k, n_fsdp) for k in range(1, half)]
+    mate = f + 1 - 2 * lax.rem(f, 2)
+    for there in line:
+        remote(g_ref, g.at[f], g_sem, 0, (b, there)).start()
     g[f] = g_ref[...]
     q_all[0:4] = q_ref[...]
-    load_w.wait()
-    load_h.wait()
+    block = g_ref.shape[0]
+    per_tile = g_pad.shape[0] // block
+    g_pad[...] = jnp.zeros_like(g_pad)
+    g_pad[pl.ds(pl.multiple_of(block * lax.rem(f, per_tile), block), block)] = g_ref[...]
     send_q.wait_recv()
     q_all[4:8] = q_left[...]
     q = q_all[...]
-
-    def gather_g():
-        settle(g.at[pl.ds(0, n_fsdp - 1)], g_sem.at[1])
+    gq[f] = joined(mm(pieces(q), g_pad[...], NT))
+    for where in others:
+        remote(gq.at[f], gq.at[f], gq_sem, 0, where).start()
+    load_w.wait()
+    load_h.wait()
+    tokens = None
 
     for r in range(ROUNDS):
         q3 = pieces(q)
         own = joined(mm(q3, w[...], NT))
         if r == 0:
-            gather_g()
-        tokens = g[...].reshape(n_fsdp * g.shape[1], width)
-        own = own - joined(mm(pieces(step * joined(mm(q3, tokens, NT))), h[...], NN))
+            settle(gq.at[pl.ds(0, n_fsdp - 1)], gq_sem.at[1])
+            seen = jnp.concatenate(
+                [sum(gq[i + k] for k in range(per_tile)) for i in range(0, n_fsdp, per_tile)], axis=1
+            )
+        else:
+            seen = joined(mm(q3, tokens, NT))
+        own = own - joined(mm(pieces(step * seen), h[...], NN))
         p_send[r, 0] = own[0:4]
         p_send[r, 1] = own[4:8]
         to_up = remote(p_send.at[r, 0], p_recv.at[r, 1], p_sem, 4 * r, (up, f))
@@ -125,13 +136,17 @@
         to_up.start()
         to_down.start()
         if r == 0:
-            for i in range(0, rows, 128):
-                base[i : i + 128] = w[i : i + 128].astype(F32) - step * mm(h[:, i : i + 128], tokens, TN)
+            settle(g.at[pl.ds(0, half - 1)], g_sem.at[1])
+            for there in [f] + line:
+                remote(g.at[there], g.at[there], g_sem, 2, (b, mate)).start()
         to_up.wait_recv()
         to_down.wait_recv()
         p = jnp.concatenate([own[0:4] - p_recv[r, 0], p_recv[r, 1] - own[4:8]], axis=0)
         p3 = pieces(p)
         part = joined(mm(p3, w[...], NN))
+        if r == 0:
+            settle(g.at[pl.ds(0, half)], g_sem.at[3])
+            tokens = g[...].reshape(n_fsdp * block, width)
         part = part - joined(mm(pieces(step * joined(mm(p3, h[...], NT))), tokens, NN))
         for s in range(half):
             i, j = 4 * (s // (half // 2)), strip * (s % (half // 2))
@@ -143,6 +158,9 @@
             to = lax.rem(mine + k, half)
             remote(m_part.at[r, to], m_recv.at[r, mine], rs_sem, 2 * r, (b, start_of_half + to)).start()
         m_recv[r, mine] = m_part[r, mine]
+        if r == 0:
+            for i in range(0, rows, 128):
+                base[i : i + 128] = w[i : i + 128].astype(F32) - step * mm(h[:, i : i + 128], tokens, TN)
         settle(m_recv.at[r, pl.ds(0, 2 * half - 1)], rs_sem.at[2 * r + 1])
         total = m_recv[r, 0] - m_recv[r, half]
         for s in range(1, half):
@@ -167,7 +185,9 @@
     right[...] = jnp.concatenate([q3[0:8], q3[8:16], q3[0:8], q3[16:24], q3[0:8], q3[8:16]], axis=0)
 
     send_q.wait_send()
-    settle(g.at[pl.ds(0, n_fsdp - 1)], g_sem.at[0])
+    settle(gq.at[pl.ds(0, n_fsdp - 1)], gq_sem.at[0])
+    settle(g.at[pl.ds(0, half - 1)], g_sem.at[0])
+    settle(g.at[pl.ds(0, half)], g_sem.at[2])
     for r in range(ROUNDS):
         settle(p_send.at[r, 0], p_sem.at[4 * r])
         settle(p_send.at[r, 1], p_sem.at[4 * r + 2])
@@ -212,6 +232,8 @@
             pltpu.VMEM((tokens, rows), BF16),
             pltpu.VMEM((n_fsdp, tokens // n_fsdp, width), BF16),
             pltpu.VMEM((tokens // n_fsdp, width), BF16),
+            pltpu.VMEM((128, width), BF16),
+            pltpu.VMEM((n_fsdp, 2 * rank, 128), F32),
             pltpu.VMEM((rank, width), F32),
             pltpu.VMEM((rank, width), F32),
             pltpu.VMEM((2 * rank, width), F32),
@@ -224,6 +246,7 @@
             dma((4,)),
             dma((2,)),
             dma((2,)),
+            dma((4,)),
             dma((4 * ROUNDS,)),
             dma((2 * ROUNDS,)),
             dma((2 * ROUNDS,)),

time: 69.3 us -> 66.3 us (0.957)
  the two profiles are of different devices: /device:TPU:40 before, /device:TPU:8 now
where the time goes in v3:
time: 66.3 us; the launch traced here: 66.2 us
  Pallas kernels  65.6 us (99%)
    pallas_call x1, Pallas kernels, on_device(): pl.pallas_call(functools.partial(kernel, n_blk, n_fsdp, 0.5 / math.sqrt(t...  63.8 us
    pallas_call x1, Pallas kernels, on_device(): pl.pallas_call(write_kernel, out_shape=(jax.ShapeDtypeStruct((rows, width...  1.74 us

profile of v3, /device:TPU:8, one launch (start us, length us, event | category | flops | bytes accessed | tf_op | source)
XLA Modules:
  0.0 66.2 jit_solution(14317030913307498482)
XLA Ops:
  0.6 63.8 %shard_map.59 = (f32[768,1536]{1,0:T(8,128)S(1)}, bf16[48,768]{1,0:T(8,128)(2,1)S(1)}, bf16[48,1536]{1,0:T(8,128)(2,1)S(1)}, f32[4,1536]{1,0:T(4,128)S(1)}) custom-call(bf16[768,1536]{1,0:T(8,128)(2,1)} %bitcast.10, bf16[256,768]{1,0:T(8,128)(2,1)} %bitcast.11, bf16[16,1536]{1,0:T(8,128)(2,1)} %bitcast.12, f32[4,1536]{1,0:T(4,128)} %bitcast.13), custom_call_target="tpu_custom_call" | custom-call | tf_op jit(solution)/shard_map/pallas_call | solution.py:220
  64.5 1.7 %shard_map.60 = (bf16[768,1536]{1,0:T(8,128)(2,1)}, f32[4,1536]{1,0:T(4,128)}) custom-call(f32[768,1536]{1,0:T(8,128)S(1)} %get-tuple-element.8.base, bf16[48,768]{1,0:T(8,128)(2,1)S(1)} %get-tuple-element.9.left, bf16[48,1536]{1,0:T(8,128)(2,1)S(1)} %get-tuple-element.10.right, f32[4,1536]{1,0:T(4,128)S(1)} %get-tuple-element.11.edge), custom_call_target="tpu_custom_call" | custom-call | tf_op jit(solution)/shard_map/pallas_call | solution.py:258

commit v4 on v3

--- a/solution.py
+++ b/solution.py
@@ -87,9 +87,12 @@
     load_q = pltpu.make_async_copy(q_hbm, q_ref, in_sem.at[3])
     for load in (load_q, load_g, load_w, load_h):
         load.start()
-    others = [(b, lax.rem(f + k, n_fsdp)) for k in range(1, n_fsdp)]
+    others = [(b, lax.rem(f + k, n_fsdp)) for k in sorted(range(1, n_fsdp), key=lambda k: abs(k - half))]
     barrier = pltpu.get_barrier_semaphore()
-    beside = [(there, start_of_half + s) for there in (up, down) for s in range(half)]
+    odd = lax.rem(mine, 2)
+    mainly, also = jnp.where(odd == 1, up, down), jnp.where(odd == 1, down, up)
+    beside = [(mainly, start_of_half + s) for s in range(half)]
+    beside += [(also, start_of_half + 2 * s + odd) for s in range(half // 2)]
     for where in others + beside:
         pl.semaphore_signal(barrier, inc=1, device_id=where, device_id_type=MESH)
     pl.semaphore_wait(barrier, len(others) + len(beside))
@@ -98,10 +101,20 @@
     load_g.wait()
     send_q = remote(q_ref, q_left, q_sem, 0, (up, f))
     send_q.start()
-    line = [lax.rem(f + 2 * k, n_fsdp) for k in range(1, half)]
     mate = f + 1 - 2 * lax.rem(f, 2)
-    for there in line:
+
+    def along_z(k):
+        return lax.rem(f + 2 * k + n_fsdp, n_fsdp)
+
+    def pass_to_mate(owners):
+        for there in owners:
+            remote(g.at[there], g.at[there], g_sem, 4, (b, mate)).start()
+
+    near = [along_z(k) for k in (1, -1, 2, -2)]
+    far = [along_z(k) for k in (3, -3, 4)]
+    for there in near:
         remote(g_ref, g.at[f], g_sem, 0, (b, there)).start()
+    remote(g_ref, g.at[f], g_sem, 4, (b, mate)).start()
     g[f] = g_ref[...]
     q_all[0:4] = q_ref[...]
     block = g_ref.shape[0]
@@ -114,20 +127,26 @@
     gq[f] = joined(mm(pieces(q), g_pad[...], NT))
     for where in others:
         remote(gq.at[f], gq.at[f], gq_sem, 0, where).start()
+    settle(g.at[pl.ds(0, len(near))], g_sem.at[1])
+    for held, to in ((2, -1), (-2, 1), (2, -2)):
+        held = along_z(held)
+        remote(g.at[held], g.at[held], g_sem, 2, (b, along_z(to))).start()
+    pass_to_mate(near)
     load_w.wait()
     load_h.wait()
     tokens = None
 
     for r in range(ROUNDS):
         q3 = pieces(q)
-        own = joined(mm(q3, w[...], NT))
         if r == 0:
+            own = joined(mm(q3, w[...], NT))
             settle(gq.at[pl.ds(0, n_fsdp - 1)], gq_sem.at[1])
             seen = jnp.concatenate(
                 [sum(gq[i + k] for k in range(per_tile)) for i in range(0, n_fsdp, per_tile)], axis=1
             )
         else:
             seen = joined(mm(q3, tokens, NT))
+            own = joined(mm(q3, w[...], NT))
         own = own - joined(mm(pieces(step * seen), h[...], NN))
         p_send[r, 0] = own[0:4]
         p_send[r, 1] = own[4:8]
@@ -136,24 +155,25 @@
         to_up.start()
         to_down.start()
         if r == 0:
-            settle(g.at[pl.ds(0, half - 1)], g_sem.at[1])
-            for there in [f] + line:
-                remote(g.at[there], g.at[there], g_sem, 2, (b, mate)).start()
+            settle(g.at[pl.ds(0, len(far))], g_sem.at[3])
+            pass_to_mate(far)
         to_up.wait_recv()
         to_down.wait_recv()
         p = jnp.concatenate([own[0:4] - p_recv[r, 0], p_recv[r, 1] - own[4:8]], axis=0)
         p3 = pieces(p)
+        seen = joined(mm(p3, h[...], NT))
         part = joined(mm(p3, w[...], NN))
         if r == 0:
-            settle(g.at[pl.ds(0, half)], g_sem.at[3])
+            settle(g.at[pl.ds(0, half)], g_sem.at[5])
             tokens = g[...].reshape(n_fsdp * block, width)
-        part = part - joined(mm(pieces(step * joined(mm(p3, h[...], NT))), tokens, NN))
+        part = part - joined(mm(pieces(step * seen), tokens, NN))
         for s in range(half):
-            i, j = 4 * (s // (half // 2)), strip * (s % (half // 2))
+            i, j = 4 - 4 * (s % 2), strip * (s // 2)
             m_part[r, s] = part[i : i + 4, j : j + strip]
         for s in range(half // 2):
-            remote(m_part.at[r, s], m_recv.at[r, half + mine], rs_sem, 2 * r, (up, start_of_half + half // 2 + s)).start()
-            remote(m_part.at[r, half // 2 + s], m_recv.at[r, half + mine], rs_sem, 2 * r, (down, start_of_half + s)).start()
+            above, below = 2 * s + 1, 2 * s
+            remote(m_part.at[r, above], m_recv.at[r, half + mine], rs_sem, 2 * r, (up, start_of_half + below)).start()
+            remote(m_part.at[r, below], m_recv.at[r, half + mine], rs_sem, 2 * r, (down, start_of_half + above)).start()
         for k in range(1, half):
             to = lax.rem(mine + k, half)
             remote(m_part.at[r, to], m_recv.at[r, mine], rs_sem, 2 * r, (b, start_of_half + to)).start()
@@ -165,12 +185,12 @@
         total = m_recv[r, 0] - m_recv[r, half]
         for s in range(1, half):
             total = total + (m_recv[r, s] - m_recv[r, half + s])
-        m_sum[r, f] = jnp.where(mine < half // 2, 1.0, -1.0) * total
+        m_sum[r, f] = jnp.where(odd == 1, 1.0, -1.0) * total
         for where in others:
             remote(m_sum.at[r, f], m_sum.at[r, f], ag_sem, 2 * r, where).start()
         settle(m_sum.at[r, pl.ds(0, n_fsdp - 1)], ag_sem.at[2 * r + 1])
         for s in range(half):
-            i, j = 4 * (s // (half // 2)), strip * (s % (half // 2))
+            i, j = 4 - 4 * (s % 2), strip * (s // 2)
             m_all[i : i + 4, j : j + strip] = m_sum[r, s] + m_sum[r, half + s]
         m = m_all[...]
         if r < ROUNDS - 1:
@@ -186,8 +206,9 @@
 
     send_q.wait_send()
     settle(gq.at[pl.ds(0, n_fsdp - 1)], gq_sem.at[0])
-    settle(g.at[pl.ds(0, half - 1)], g_sem.at[0])
-    settle(g.at[pl.ds(0, half)], g_sem.at[2])
+    settle(g.at[pl.ds(0, len(near))], g_sem.at[0])
+    settle(g.at[pl.ds(0, len(far))], g_sem.at[2])
+    settle(g.at[pl.ds(0, half)], g_sem.at[4])
     for r in range(ROUNDS):
         settle(p_send.at[r, 0], p_sem.at[4 * r])
         settle(p_send.at[r, 1], p_sem.at[4 * r + 2])
@@ -246,7 +267,7 @@
             dma((4,)),
             dma((2,)),
             dma((2,)),
-            dma((4,)),
+            dma((6,)),
             dma((4 * ROUNDS,)),
             dma((2 * ROUNDS,)),
             dma((2 * ROUNDS,)),

time: 66.3 us -> 59.9 us (0.903)
  Pallas kernels: 65.6 us -> 59.2 us
    pallas_call x1, Pallas kernels: 63.8 us -> 57.4 us  [on_device(): pl.pallas_call(functools.partial(kernel, n_blk, n_fsdp, 0.5 / math.sqrt(t...]
where the time goes in v4:
time: 59.9 us; the launch traced here: 59.8 us
  Pallas kernels  59.2 us (99%)
  between operations  0.64 us (1%)
    pallas_call x1, Pallas kernels, on_device(): pl.pallas_call(functools.partial(kernel, n_blk, n_fsdp, 0.5 / math.sqrt(t...  57.4 us
    pallas_call x1, Pallas kernels, on_device(): pl.pallas_call(write_kernel, out_shape=(jax.ShapeDtypeStruct((rows, width...  1.75 us

profile of v4, /device:TPU:8, one launch (start us, length us, event | category | flops | bytes accessed | tf_op | source)
XLA Modules:
  0.0 59.8 jit_solution(312749661594500181)
XLA Ops:
  0.6 57.4 %shard_map.59 = (f32[768,1536]{1,0:T(8,128)S(1)}, bf16[48,768]{1,0:T(8,128)(2,1)S(1)}, bf16[48,1536]{1,0:T(8,128)(2,1)S(1)}, f32[4,1536]{1,0:T(4,128)S(1)}) custom-call(bf16[768,1536]{1,0:T(8,128)(2,1)} %bitcast.10, bf16[256,768]{1,0:T(8,128)(2,1)} %bitcast.11, bf16[16,1536]{1,0:T(8,128)(2,1)} %bitcast.12, f32[4,1536]{1,0:T(4,128)} %bitcast.13), custom_call_target="tpu_custom_call" | custom-call | tf_op jit(solution)/shard_map/pallas_call | solution.py:241
  58.1 1.8 %shard_map.60 = (bf16[768,1536]{1,0:T(8,128)(2,1)}, f32[4,1536]{1,0:T(4,128)}) custom-call(f32[768,1536]{1,0:T(8,128)S(1)} %get-tuple-element.8.base, bf16[48,768]{1,0:T(8,128)(2,1)S(1)} %get-tuple-element.9.left, bf16[48,1536]{1,0:T(8,128)(2,1)S(1)} %get-tuple-element.10.right, f32[4,1536]{1,0:T(4,128)S(1)} %get-tuple-element.11.edge), custom_call_target="tpu_custom_call" | custom-call | tf_op jit(solution)/shard_map/pallas_call | solution.py:279

commit v5 on v4

--- a/solution.py
+++ b/solution.py
@@ -62,7 +62,7 @@
 
 
 def kernel(n_blk, n_fsdp, step, w_hbm, h_hbm, g_hbm, q_hbm, base, left, right, edge_ref,
-           w, h, g, g_ref, g_pad, gq, q_ref, q_left, q_all, p_send, p_recv, m_part, m_recv, m_sum,
+           w, h, g, w_t, tokens_t, g_ref, g_pad, gq, q_ref, q_left, q_all, p_send, p_recv, m_part, m_recv, m_sum,
            m_all, in_sem, q_sem, gq_sem, g_sem, p_sem, rs_sem, ag_sem):
     b, f = lax.axis_index("blk"), lax.axis_index("fsdp")
     up, down = lax.rem(b + 1, n_blk), lax.rem(b + n_blk - 1, n_blk)
@@ -137,17 +137,19 @@
     tokens = None
 
     for r in range(ROUNDS):
-        q3 = pieces(q)
         if r == 0:
-            own = joined(mm(q3, w[...], NT))
+            own = joined(mm(pieces(q), w[...], NT))
             settle(gq.at[pl.ds(0, n_fsdp - 1)], gq_sem.at[1])
             seen = jnp.concatenate(
                 [sum(gq[i + k] for k in range(per_tile)) for i in range(0, n_fsdp, per_tile)], axis=1
             )
         else:
-            seen = joined(mm(q3, tokens, NT))
-            own = joined(mm(q3, w[...], NT))
+            m3 = pieces(m)
+            seen = joined(mm(m3, tokens_t[...], NN))
+            own = joined(mm(m3, w_t[...], NN))
         own = own - joined(mm(pieces(step * seen), h[...], NN))
+        if r > 0:
+            q, own = eliminate(q, m, [own])
         p_send[r, 0] = own[0:4]
         p_send[r, 1] = own[4:8]
         to_up = remote(p_send.at[r, 0], p_recv.at[r, 1], p_sem, 4 * r, (up, f))
@@ -181,6 +183,8 @@
         if r == 0:
             for i in range(0, rows, 128):
                 base[i : i + 128] = w[i : i + 128].astype(F32) - step * mm(h[:, i : i + 128], tokens, TN)
+            w_t[...] = w[...].T
+            tokens_t[...] = tokens.T
         settle(m_recv.at[r, pl.ds(0, 2 * half - 1)], rs_sem.at[2 * r + 1])
         total = m_recv[r, 0] - m_recv[r, half]
         for s in range(1, half):
@@ -193,11 +197,8 @@
             i, j = 4 - 4 * (s % 2), strip * (s // 2)
             m_all[i : i + 4, j : j + strip] = m_sum[r, s] + m_sum[r, half + s]
         m = m_all[...]
-        if r < ROUNDS - 1:
-            (q,) = eliminate(q, m, [])
-        else:
-            q, p = eliminate(q, m, [p])
-
+
+    q, p = eliminate(q, m, [p])
     edge_ref[...] = q[0:4]
     sign = jnp.where(lax.broadcasted_iota(jnp.int32, (8, 1), 0) < 4, -0.5, 0.5)
     q3, p3 = pieces(q), pieces(sign * p)
@@ -252,6 +253,8 @@
             pltpu.VMEM((rows, width), BF16),
             pltpu.VMEM((tokens, rows), BF16),
             pltpu.VMEM((n_fsdp, tokens // n_fsdp, width), BF16),
+            pltpu.VMEM((width, rows), BF16),
+            pltpu.VMEM((width, tokens), BF16),
             pltpu.VMEM((tokens // n_fsdp, width), BF16),
             pltpu.VMEM((128, width), BF16),
             pltpu.VMEM((n_fsdp, 2 * rank, 128), F32),

time: 59.9 us -> 59.5 us (level)
  no operation moved by 1% of the time
where the time goes in v5:
time: 59.5 us; the launch traced here: 59.3 us
  Pallas kernels  58.7 us (99%)
  between operations  0.64 us (1%)
    pallas_call x1, Pallas kernels, on_device(): pl.pallas_call(functools.partial(kernel, n_blk, n_fsdp, 0.5 / math.sqrt(t...  57 us
    pallas_call x1, Pallas kernels, on_device(): pl.pallas_call(write_kernel, out_shape=(jax.ShapeDtypeStruct((rows, width...  1.74 us

profile of v5, /device:TPU:8, one launch (start us, length us, event | category | flops | bytes accessed | tf_op | source)
XLA Modules:
  0.0 59.3 jit_solution(14134857047229509252)
XLA Ops:
  0.6 57.0 %shard_map.59 = (f32[768,1536]{1,0:T(8,128)S(1)}, bf16[48,768]{1,0:T(8,128)(2,1)S(1)}, bf16[48,1536]{1,0:T(8,128)(2,1)S(1)}, f32[4,1536]{1,0:T(4,128)S(1)}) custom-call(bf16[768,1536]{1,0:T(8,128)(2,1)} %bitcast.10, bf16[256,768]{1,0:T(8,128)(2,1)} %bitcast.11, bf16[16,1536]{1,0:T(8,128)(2,1)} %bitcast.12, f32[4,1536]{1,0:T(4,128)} %bitcast.13), custom_call_target="tpu_custom_call" | custom-call | tf_op jit(solution)/shard_map/pallas_call | solution.py:242
  57.6 1.7 %shard_map.60 = (bf16[768,1536]{1,0:T(8,128)(2,1)}, f32[4,1536]{1,0:T(4,128)}) custom-call(f32[768,1536]{1,0:T(8,128)S(1)} %get-tuple-element.8.base, bf16[48,768]{1,0:T(8,128)(2,1)S(1)} %get-tuple-element.9.left, bf16[48,1536]{1,0:T(8,128)(2,1)S(1)} %get-tuple-element.10.right, f32[4,1536]{1,0:T(4,128)S(1)} %get-tuple-element.11.edge), custom_call_target="tpu_custom_call" | custom-call | tf_op jit(solution)/shard_map/pallas_call | solution.py:282

commit v6 on v5

--- a/solution.py
+++ b/solution.py
@@ -93,14 +93,14 @@
     mainly, also = jnp.where(odd == 1, up, down), jnp.where(odd == 1, down, up)
     beside = [(mainly, start_of_half + s) for s in range(half)]
     beside += [(also, start_of_half + 2 * s + odd) for s in range(half // 2)]
-    for where in others + beside:
+    for where in beside + others:
         pl.semaphore_signal(barrier, inc=1, device_id=where, device_id_type=MESH)
     pl.semaphore_wait(barrier, len(others) + len(beside))
 
     load_q.wait()
-    load_g.wait()
     send_q = remote(q_ref, q_left, q_sem, 0, (up, f))
     send_q.start()
+    load_g.wait()
     mate = f + 1 - 2 * lax.rem(f, 2)
 
     def along_z(k):

time: 59.5 us -> 59.4 us (level)
  no operation moved by 1% of the time
where the time goes in v6:
time: 59.4 us; the launch traced here: 59.3 us
  Pallas kernels  58.6 us (99%)
  between operations  0.64 us (1%)
    pallas_call x1, Pallas kernels, on_device(): pl.pallas_call(functools.partial(kernel, n_blk, n_fsdp, 0.5 / math.sqrt(t...  56.9 us
    pallas_call x1, Pallas kernels, on_device(): pl.pallas_call(write_kernel, out_shape=(jax.ShapeDtypeStruct((rows, width...  1.74 us

profile of v6, /device:TPU:8, one launch (start us, length us, event | category | flops | bytes accessed | tf_op | source)
XLA Modules:
  0.0 59.3 jit_solution(10029476159401580764)
XLA Ops:
  0.6 56.9 %shard_map.59 = (f32[768,1536]{1,0:T(8,128)S(1)}, bf16[48,768]{1,0:T(8,128)(2,1)S(1)}, bf16[48,1536]{1,0:T(8,128)(2,1)S(1)}, f32[4,1536]{1,0:T(4,128)S(1)}) custom-call(bf16[768,1536]{1,0:T(8,128)(2,1)} %bitcast.10, bf16[256,768]{1,0:T(8,128)(2,1)} %bitcast.11, bf16[16,1536]{1,0:T(8,128)(2,1)} %bitcast.12, f32[4,1536]{1,0:T(4,128)} %bitcast.13), custom_call_target="tpu_custom_call" | custom-call | tf_op jit(solution)/shard_map/pallas_call | solution.py:242
  57.5 1.7 %shard_map.60 = (bf16[768,1536]{1,0:T(8,128)(2,1)}, f32[4,1536]{1,0:T(4,128)}) custom-call(f32[768,1536]{1,0:T(8,128)S(1)} %get-tuple-element.8.base, bf16[48,768]{1,0:T(8,128)(2,1)S(1)} %get-tuple-element.9.left, bf16[48,1536]{1,0:T(8,128)(2,1)S(1)} %get-tuple-element.10.right, f32[4,1536]{1,0:T(4,128)S(1)} %get-tuple-element.11.edge), custom_call_target="tpu_custom_call" | custom-call | tf_op jit(solution)/shard_map/pallas_call | solution.py:282
